TPU v7x, 32 devices: a whole 2x2x4 slice. The times are simulated.
32 devices in a mesh: parts: 2 (over x), rows: 16 (over z, y, core).
Axes of the slice: x: 2, y: 2, z: 4, core: 2. Of those that a mesh axis runs over, the one named last changes fastest.
Arguments:
- gain_tiles: float32 [4, 8192, 3, 128], P(None, ('parts', 'rows')), parts along dimension 1, may hold values from -0.21875 to 0.21875
- tile_pattern: int32 [8, 32, 3], P('parts'), parts along dimension 0, may hold values from 0 to 31, as said below
- offset_terms: float32 [4, 8192], P(None, ('parts', 'rows')), parts along dimension 1, may hold values from -6 to 6
- last_mean: float32 [8192], P(('parts', 'rows')), parts along dimension 0, may hold values from -6 to 6
- last_covariance: float32 [8192, 4096], P(('parts', 'rows')), parts along dimension 0, as said below
- noise_covariance: float32 [4, 8192, 4096], P(None, ('parts', 'rows')), parts along dimension 1, as said below
Outputs:
- smoothed_covariance: float32 [4, 8192, 4096], P(None, ('parts', 'rows')), parts along dimension 1
- smoothed_mean: float32 [4, 8192], P(None, ('parts', 'rows')), parts along dimension 1
There are 2 independent parts, one for each index of `parts`. A program takes and returns all parts, laid end to end along the dimension named above; each array names one. Nothing has to cross between parts.
Inputs may be any that keep to these rules, and one draw needn't show every extreme that they name: `tile_pattern`: each tile row names 3 different tile columns; the first is the tile row's own number. `last_covariance`: symmetric. `noise_covariance`: each block's matrix is symmetric.
All inputs are finite; a program needn't handle non-finite values.
Results may differ from a plain program's by a relative error of at most 0.0001.
Values sent between devices are 32-bit elements; how exact they have to be, the bound alone decides.
A program may use at most 192 MiB of HBM per device.

v0:
```python
import jax
import jax.numpy as jnp
from jax import lax
from jax.sharding import PartitionSpec as P

WIDTH = 4096
TILE = 128
PER_ROW = 3
BLOCKS = 4
TILE_ROWS = 32


def right_product(dense_rows, gain_values, pattern_block):
    row_count = dense_rows.shape[0]
    tiled = dense_rows.reshape(row_count, TILE_ROWS, TILE)
    picked = tiled[:, pattern_block, :]
    shaped = gain_values.reshape(TILE_ROWS, TILE, PER_ROW, TILE)
    result = jnp.einsum("rtkj,tckj->rtc", picked, shaped, precision=lax.Precision.HIGHEST)
    return result.reshape(row_count, WIDTH)


def left_product(columns, gain_values, pattern_block):
    column_count = columns.shape[1]
    tiled = columns.reshape(TILE_ROWS, TILE, column_count)
    picked = tiled[pattern_block]
    shaped = gain_values.reshape(TILE_ROWS, TILE, PER_ROW, TILE)
    result = jnp.einsum("tkjc,tqkj->ctq", picked, shaped, precision=lax.Precision.HIGHEST)
    return result.reshape(column_count, WIDTH)


def shards(gain_tiles, tile_pattern, offset_terms, last_mean, last_covariance, noise_covariance):
    local_rows = last_mean.shape[0]
    first_row = lax.axis_index("rows") * local_rows
    row_numbers = first_row + jnp.arange(local_rows, dtype=jnp.int32)
    tile_match = (
        row_numbers[:, None] // TILE == jnp.arange(TILE_ROWS, dtype=jnp.int32)[None, :]
    ).astype(jnp.int32)
    current_mean = last_mean
    covariance = last_covariance
    cov_list = []
    mean_list = []
    for block_index in reversed(range(BLOCKS)):
        pattern_block = tile_pattern[block_index]
        gain_values = lax.all_gather(gain_tiles[block_index], "rows", axis=0, tiled=True)
        partial_image = right_product(covariance, gain_values, pattern_block)
        received = lax.all_to_all(partial_image, "rows", split_axis=1, concat_axis=0, tiled=True)
        covariance = (
            left_product(received, gain_values, pattern_block) + noise_covariance[block_index]
        )
        cov_list.append(covariance)
        gathered_mean = lax.all_gather(current_mean, "rows", axis=0, tiled=True)
        mean_tiles = gathered_mean.reshape(TILE_ROWS, TILE)
        own_pattern = jnp.sum(tile_match[:, :, None] * pattern_block[None, :, :], axis=1)
        picked = mean_tiles[own_pattern]
        current_mean = (
            jnp.sum(picked * gain_tiles[block_index], axis=(1, 2)) + offset_terms[block_index]
        )
        mean_list.append(current_mean)
    cov_list = cov_list[::-1]
    mean_list = mean_list[::-1]
    return (jnp.stack(cov_list, 0), jnp.stack(mean_list, 0))


def solution(mesh):
    in_specs = (
        P(None, ("parts", "rows"), None, None),
        P("parts", None, None),
        P(None, ("parts", "rows")),
        P(("parts", "rows")),
        P(("parts", "rows"), None),
        P(None, ("parts", "rows"), None),
    )
    out_specs = (P(None, ("parts", "rows"), None), P(None, ("parts", "rows")))
    return jax.shard_map(shards, mesh=mesh, in_specs=in_specs, out_specs=out_specs, check_vma=False)
```

profile of v0, /device:TPU:0, one launch (start us, length us, event | category | flops | bytes accessed | tf_op | source)
XLA Modules:
  0.0 974.5 jit_solution(8600243610957248146)
XLA Ops:
  7.2 2.6 fusion.25
  10.5 5.6 copy.137
  16.1 5.6 copy.139
  22.0 11.3 %gather_fusion = f32[96,256,128]{2,1,0:T(8,128)} fusion(f32[256,32,128]{2,0,1:T(8,128)} %copy.139, s32[1024]{0:T(1024)S(1)} %pad_clamp_fusion.7), kind=kCustom, calls=%fused_computation | custom fusion | bytes 25166208 | tf_op jit(solution)/shard_map/gather | solution.py:16
  33.3 41.6 %all-gather.13.cloned.1.call-done = f32[1,4096,3,128]{3,1,2,0:T(8,128)} async-done(((f32[1,256,3,128]{3,1,2,0:T(8,128)}), f32[1,4096,3,128]{3,1,2,0:T(8,128)}) %all-gather.13.cloned.1.call-update) | async-done | bytes 6291472 | tf_op jit(solution)/shard_map/all_gather | solution.py:44
  74.9 21.4 %fusion.17 = f32[32,256,128,1]{1,2,3,0:T(8,128)} fusion(f32[256,32,3,128]{3,0,2,1:T(8,128)} %bitcast.173, f32[32,128,3,128]{3,1,0,2:T(8,128)} %bitcast.184), kind=kOutput, calls=%fused_computation.30 | convolution fusion | flops 4831838208 | bytes 23068672 | tf_op jit(solution)/shard_map/rtkj,tckj->rtc/dot_general | solution.py:18
  96.3 5.4 copy.141
  101.7 4.5 all-to-all-start
  107.0 9.8 %fusion.24 = (f32[1,256,4096]{2,1,0:T(8,128)}, f32[1,256,4096]{2,1,0:T(8,128)}, f32[1,256,4096]{2,1,0:T(8,128)}) fusion(f32[4,256,4096]{2,1,0:T(8,128)} %param.11), kind=kLoop, calls=%fused_computation.82 | loop fusion | bytes 25165824 | tf_op jit(solution)/shard_map/slice | solution.py:48
  116.8 5.6 copy.143
  122.6 97.4 %all-to-all-done = f32[256,16,256]{2,0,1:T(8,128)} async-done(((f32[256,16,256]{2,0,1:T(8,128)}), f32[256,16,256]{2,0,1:T(8,128)}, u32[]{:S(2)}, u32[]{:S(2)}) %all-to-all-start) | async-done | bytes 4194336 | tf_op jit(solution)/shard_map/all_to_all | solution.py:46
  220.0 11.1 %gather_fusion.1 = f32[96,128,256]{2,1,0:T(8,128)} fusion(f32[32,128,256]{2,1,0:T(8,128)} %bitcast.10, s32[1024]{0:T(1024)S(1)} %pad_clamp_fusion.7), kind=kCustom, calls=%fused_computation.1 | custom fusion | bytes 25166208 | tf_op jit(solution)/shard_map/gather | solution.py:25
  231.1 15.4 %bitcast_add_fusion = (f32[256,32,128]{0,2,1:T(8,128)}, f32[32,256,128,1]{1,2,3,0:T(8,128)}) fusion(f32[256,32,128]{0,2,1:T(8,128)} %bitcast.190, f32[32,3,128,256]{3,2,1,0:T(8,128)} %bitcast.174, f32[32,128,3,128]{3,1,0,2:T(8,128)} %bitcast.185), kind=kOutput, calls=%fused_computation.32 | convolution fusion | flops 4832886784 | bytes 31457280 | tf_op jit(solution)/shard_map/tkjc,tqkj->ctq/dot_general | solution.py:27
  246.5 11.2 %gather_fusion.2 = f32[96,256,128]{1,2,0:T(8,128)} fusion(f32[256,32,128]{0,2,1:T(8,128)} %get-tuple-element.32, s32[1024]{0:T(1024)S(1)} %pad_clamp_fusion.6), kind=kCustom, calls=%fused_computation.2 | custom fusion | bytes 25166208 | tf_op jit(solution)/shard_map/gather | solution.py:16
  257.7 12.7 %copy.145 = f32[32,3,256,128]{3,2,1,0:T(8,128)} copy(f32[32,3,256,128]{2,3,1,0:T(8,128)} %bitcast.170) | data formatting | bytes 25165824 | tf_op jit(solution)/shard_map/gather | solution.py:16
  270.5 21.4 %fusion.4 = f32[32,256,128,1]{1,2,3,0:T(8,128)} fusion(f32[32,3,256,128]{3,2,1,0:T(8,128)} %copy.145, f32[32,128,3,128]{3,1,0,2:T(8,128)} %bitcast.182), kind=kOutput, calls=%fused_computation.17 | convolution fusion | flops 4831838208 | bytes 23068672 | tf_op jit(solution)/shard_map/rtkj,tckj->rtc/dot_general | solution.py:18
  291.9 5.4 copy.147
  297.3 40.2 %all-to-all-start.1 = ((f32[256,16,256]{2,0,1:T(8,128)}), f32[256,16,256]{2,0,1:T(8,128)}, u32[]{:S(2)}, u32[]{:S(2)}) async-start(f32[256,16,256]{2,0,1:T(8,128)} %copy.147), calls=%async_computation.1 | async-start | bytes 8388608 | tf_op jit(solution)/shard_map/all_to_all | solution.py:46
  338.1 5.8 copy.149
  344.1 108.9 %all-to-all-done.1 = f32[256,16,256]{2,0,1:T(8,128)} async-done(((f32[256,16,256]{2,0,1:T(8,128)}), f32[256,16,256]{2,0,1:T(8,128)}, u32[]{:S(2)}, u32[]{:S(2)}) %all-to-all-start.1) | async-done | bytes 4194336 | tf_op jit(solution)/shard_map/all_to_all | solution.py:46
  453.1 11.1 %gather_fusion.3 = f32[96,128,256]{2,1,0:T(8,128)} fusion(f32[32,128,256]{2,1,0:T(8,128)} %bitcast.25, s32[1024]{0:T(1024)S(1)} %pad_clamp_fusion.6), kind=kCustom, calls=%fused_computation.3 | custom fusion | bytes 25166208 | tf_op jit(solution)/shard_map/gather | solution.py:25
  464.2 15.3 %bitcast_add_fusion.1 = (f32[256,32,128]{0,2,1:T(8,128)}, f32[32,256,128,1]{1,2,3,0:T(8,128)}) fusion(f32[256,32,128]{0,2,1:T(8,128)} %bitcast.191, f32[32,3,128,256]{3,2,1,0:T(8,128)} %bitcast.175, f32[32,128,3,128]{3,1,0,2:T(8,128)} %bitcast.183), kind=kOutput, calls=%fused_computation.33 | convolution fusion | flops 4832886784 | bytes 31457280 | tf_op jit(solution)/shard_map/tkjc,tqkj->ctq/dot_general | solution.py:27
  479.4 11.1 %gather_fusion.4 = f32[96,256,128]{1,2,0:T(8,128)} fusion(f32[256,32,128]{0,2,1:T(8,128)} %get-tuple-element.34, s32[1024]{0:T(1024)S(1)} %pad_clamp_fusion.5), kind=kCustom, calls=%fused_computation.4 | custom fusion | bytes 25166208 | tf_op jit(solution)/shard_map/gather | solution.py:16
  490.5 13.0 %copy.151 = f32[32,3,256,128]{3,2,1,0:T(8,128)} copy(f32[32,3,256,128]{2,3,1,0:T(8,128)} %bitcast.171) | data formatting | bytes 25165824 | tf_op jit(solution)/shard_map/gather | solution.py:16
  503.5 21.4 %fusion.2 = f32[32,256,128,1]{1,2,3,0:T(8,128)} fusion(f32[32,3,256,128]{3,2,1,0:T(8,128)} %copy.151, f32[32,128,3,128]{3,1,0,2:T(8,128)} %bitcast.180), kind=kOutput, calls=%fused_computation.15 | convolution fusion | flops 4831838208 | bytes 23068672 | tf_op jit(solution)/shard_map/rtkj,tckj->rtc/dot_general | solution.py:18
  525.0 5.4 copy.153
  530.3 19.9 %all-to-all-start.2 = ((f32[256,16,256]{2,0,1:T(8,128)}), f32[256,16,256]{2,0,1:T(8,128)}, u32[]{:S(2)}, u32[]{:S(2)}) async-start(f32[256,16,256]{2,0,1:T(8,128)} %copy.153), calls=%async_computation.2 | async-start | bytes 8388608 | tf_op jit(solution)/shard_map/all_to_all | solution.py:46
  550.3 5.6 copy.155
  556.1 71.8 %all-to-all-done.2 = f32[256,16,256]{2,0,1:T(8,128)} async-done(((f32[256,16,256]{2,0,1:T(8,128)}), f32[256,16,256]{2,0,1:T(8,128)}, u32[]{:S(2)}, u32[]{:S(2)}) %all-to-all-start.2) | async-done | bytes 4194336 | tf_op jit(solution)/shard_map/all_to_all | solution.py:46
  627.9 11.1 %gather_fusion.5 = f32[96,128,256]{2,1,0:T(8,128)} fusion(f32[32,128,256]{2,1,0:T(8,128)} %bitcast.40, s32[1024]{0:T(1024)S(1)} %pad_clamp_fusion.5), kind=kCustom, calls=%fused_computation.5 | custom fusion | bytes 25166208 | tf_op jit(solution)/shard_map/gather | solution.py:25
  639.0 15.2 %bitcast_add_fusion.2 = (f32[256,32,128]{0,2,1:T(8,128)}, f32[32,256,128,1]{1,2,3,0:T(8,128)}) fusion(f32[256,32,128]{0,2,1:T(8,128)} %bitcast.189, f32[32,3,128,256]{3,2,1,0:T(8,128)} %bitcast.176, f32[32,128,3,128]{3,1,0,2:T(8,128)} %bitcast.181), kind=kOutput, calls=%fused_computation.34 | convolution fusion | flops 4832886784 | bytes 31457280 | tf_op jit(solution)/shard_map/tkjc,tqkj->ctq/dot_general | solution.py:27
  654.3 11.1 %gather_fusion.6 = f32[96,256,128]{1,2,0:T(8,128)} fusion(f32[256,32,128]{0,2,1:T(8,128)} %get-tuple-element.36, s32[1024]{0:T(1024)S(1)} %pad_clamp_fusion.4), kind=kCustom, calls=%fused_computation.6 | custom fusion | bytes 25166208 | tf_op jit(solution)/shard_map/gather | solution.py:16
  665.4 12.8 %copy.157 = f32[32,3,256,128]{3,2,1,0:T(8,128)} copy(f32[32,3,256,128]{2,3,1,0:T(8,128)} %bitcast.172) | data formatting | bytes 25165824 | tf_op jit(solution)/shard_map/gather | solution.py:16
  678.2 21.4 %fusion = f32[32,256,128,1]{1,2,3,0:T(8,128)} fusion(f32[32,3,256,128]{3,2,1,0:T(8,128)} %copy.157, f32[32,128,3,128]{3,1,0,2:T(8,128)} %bitcast.178), kind=kOutput, calls=%fused_computation.13 | convolution fusion | flops 4831838208 | bytes 23068672 | tf_op jit(solution)/shard_map/rtkj,tckj->rtc/dot_general | solution.py:18
  699.6 5.3 copy.159
  704.9 20.1 %all-to-all-start.3 = ((f32[256,16,256]{2,0,1:T(8,128)}), f32[256,16,256]{2,0,1:T(8,128)}, u32[]{:S(2)}, u32[]{:S(2)}) async-start(f32[256,16,256]{2,0,1:T(8,128)} %copy.159), calls=%async_computation.3 | async-start | bytes 8388608 | tf_op jit(solution)/shard_map/all_to_all | solution.py:46
  725.7 83.4 %all-gather.4 = f32[16,1,256]{2,1,0:T(1,128)S(1)} all-gather(f32[1,1,256]{2,1,0:T(1,128)S(1)} %bitcast.208), channel_id=1, replica_groups=mesh['parts'=2,'rows'=16] {'rows'}, dimensions={0}, use_global_device_ids=true | all-gather | bytes 17408 | tf_op jit(solution)/shard_map/all_gather | solution.py:51
  811.3 38.4 %all-gather.5 = f32[16,1,256]{2,1,0:T(1,128)S(1)} all-gather(f32[1,1,256]{2,1,0:T(1,128)S(1)} %bitcast.201), channel_id=1, replica_groups=mesh['parts'=2,'rows'=16] {'rows'}, dimensions={0}, use_global_device_ids=true | all-gather | bytes 17408 | tf_op jit(solution)/shard_map/all_gather | solution.py:51
  852.0 17.4 %all-gather.6 = f32[16,1,256]{2,1,0:T(1,128)S(1)} all-gather(f32[1,1,256]{2,1,0:T(1,128)S(1)} %bitcast.202), channel_id=1, replica_groups=mesh['parts'=2,'rows'=16] {'rows'}, dimensions={0}, use_global_device_ids=true | all-gather | bytes 17408 | tf_op jit(solution)/shard_map/all_gather | solution.py:51
  871.7 18.8 %all-gather.7 = f32[16,1,256]{2,1,0:T(1,128)S(1)} all-gather(f32[1,1,256]{2,1,0:T(1,128)S(1)} %bitcast.203), channel_id=1, replica_groups=mesh['parts'=2,'rows'=16] {'rows'}, dimensions={0}, use_global_device_ids=true | all-gather | bytes 17408 | tf_op jit(solution)/shard_map/all_gather | solution.py:51
  893.0 5.7 copy.164
  898.6 5.7 copy.163
  904.3 5.6 copy.162
  909.9 11.1 %gather_fusion.7 = f32[96,128,256]{2,1,0:T(8,128)} fusion(f32[32,128,256]{2,1,0:T(8,128)} %bitcast.55, s32[1024]{0:T(1024)S(1)} %pad_clamp_fusion.4), kind=kCustom, calls=%fused_computation.7 | custom fusion | bytes 25166208 | tf_op jit(solution)/shard_map/gather | solution.py:25
  921.0 14.0 %fusion.6 = f32[32,256,128,1]{1,2,3,0:T(8,128)} fusion(f32[32,3,128,256]{3,2,1,0:T(8,128)} %bitcast.177, f32[32,128,3,128]{3,1,0,2:T(8,128)} %bitcast.179), kind=kOutput, calls=%fused_computation.19 | convolution fusion | flops 4831838208 | bytes 23068672 | tf_op jit(solution)/shard_map/tkjc,tqkj->ctq/dot_general | solution.py:27
  935.0 5.6 copy.161
  940.6 16.2 %slice_add_fusion = (f32[1,256,4096]{2,1,0:T(8,128)S(1)}, f32[1,256,4096]{2,1,0:T(8,128)}, f32[1,256,4096]{2,1,0:T(8,128)}, f32[1,256,4096]{2,1,0:T(8,128)}) fusion(f32[1,256,4096]{2,1,0:T(8,128)} %copy.161, f32[4,256,4096]{2,1,0:T(8,128)} %param.11, f32[1,256,4096]{2,1,0:T(8,128)} %copy.164, f32[1,256,4096]{2,1,0:T(8,128)} %copy.163, f32[1,256,4096]{2,1,0:T(8,128)} %copy.162), kind=kLoop, calls=%fused_computation.35 | loop fusion | flops 4194304 | bytes 50331648 | tf_op jit(solution)/shard_map/add | solution.py:48
  956.8 10.7 %pad_maximum_fusion = f32[4,256,4096]{2,1,0:T(8,128)} fusion(f32[1,256,4096]{2,1,0:T(8,128)} %get-tuple-element.7, f32[1,256,4096]{2,1,0:T(8,128)} %get-tuple-element.8, f32[1,256,4096]{2,1,0:T(8,128)} %get-tuple-element.9, f32[1,256,4096]{2,1,0:T(8,128)S(1)} %get-tuple-element.6), kind=kLoop, calls=%fused_computation.12 | loop fusion | flops 12582912 | bytes 33554432 | tf_op jit(solution)/shard_map/stack | solution.py:61
  (75 shorter events, 12.6 us)
Async XLA Ops:
  7.2 67.7 %all-gather.13.cloned.1.call-start = ((), (), s32[]{:S(2)}) async-start(), calls=%async_computation.4 | async-start | bytes 6684672 | tf_op jit(solution)/shard_map/all_gather | solution.py:44
  9.8 260.7 %all-gather.15.cloned.1.call-start = ((), (), s32[]{:S(2)}) async-start(), calls=%async_computation.5 | async-start | bytes 6684672 | tf_op jit(solution)/shard_map/all_gather | solution.py:44
  16.1 5.6 copy-start.1
  101.7 118.3 %all-to-all-start = ((f32[256,16,256]{2,0,1:T(8,128)}), f32[256,16,256]{2,0,1:T(8,128)}, u32[]{:S(2)}, u32[]{:S(2)}) async-start(f32[256,16,256]{2,0,1:T(8,128)} %copy.141), calls=%async_computation | async-start | bytes 8388608 | tf_op jit(solution)/shard_map/all_to_all | solution.py:46
  106.2 397.3 %all-gather.17.cloned.1.call-start = ((), (), s32[]{:S(2)}) async-start(), calls=%async_computation.6 | async-start | bytes 6684672 | tf_op jit(solution)/shard_map/all_gather | solution.py:44
  297.3 155.8 %all-to-all-start.1 = ((f32[256,16,256]{2,0,1:T(8,128)}), f32[256,16,256]{2,0,1:T(8,128)}, u32[]{:S(2)}, u32[]{:S(2)}) async-start(f32[256,16,256]{2,0,1:T(8,128)} %copy.147), calls=%async_computation.1 | async-start | bytes 8388608 | tf_op jit(solution)/shard_map/all_to_all | solution.py:46
  337.5 340.6 %all-gather.19.cloned.1.call-start = ((), (), s32[]{:S(2)}) async-start(), calls=%async_computation.7 | async-start | bytes 6684672 | tf_op jit(solution)/shard_map/all_gather | solution.py:44
  530.3 97.6 %all-to-all-start.2 = ((f32[256,16,256]{2,0,1:T(8,128)}), f32[256,16,256]{2,0,1:T(8,128)}, u32[]{:S(2)}, u32[]{:S(2)}) async-start(f32[256,16,256]{2,0,1:T(8,128)} %copy.153), calls=%async_computation.2 | async-start | bytes 8388608 | tf_op jit(solution)/shard_map/all_to_all | solution.py:46
  704.9 20.1 %copy-start.2 = (s32[4,32,3]{1,0,2:T(4,128)S(1)}, s32[4,32,3]{1,0,2:T(4,128)}, u32[]{:S(2)}) copy-start(s32[4,32,3]{1,0,2:T(4,128)} %param.7) | copy-start | bytes 4612
  704.9 20.7 %copy-start.4 = (f32[256]{0:T(256)S(1)}, f32[256]{0:T(256)}, u32[]{:S(2)}) copy-start(f32[256]{0:T(256)} %param.9) | copy-start | bytes 3076
  704.9 106.2 %copy-start = (f32[4,256,3,128]{3,1,2,0:T(8,128)S(1)}, f32[4,256,3,128]{3,1,2,0:T(8,128)}, u32[]{:S(2)}) copy-start(f32[4,256,3,128]{3,1,2,0:T(8,128)} %param.6) | copy-start | bytes 4718596
  704.9 106.3 %copy-start.3 = (f32[4,256]{1,0:T(4,128)S(1)}, f32[4,256]{1,0:T(4,128)}, u32[]{:S(2)}) copy-start(f32[4,256]{1,0:T(4,128)} %param.8) | copy-start | bytes 12292
  704.9 205.0 %all-to-all-start.3 = ((f32[256,16,256]{2,0,1:T(8,128)}), f32[256,16,256]{2,0,1:T(8,128)}, u32[]{:S(2)}, u32[]{:S(2)}) async-start(f32[256,16,256]{2,0,1:T(8,128)} %copy.159), calls=%async_computation.3 | async-start | bytes 8388608 | tf_op jit(solution)/shard_map/all_to_all | solution.py:46
Sparse Core Ops, SparseCore 0:
  10.2 64.6 all-gather.12
  77.0 95.2 all-gather.14
  174.5 88.5 all-gather.16
  340.2 108.7 all-gather.18
where the time goes:
time: 979 us; the launch traced here: 974 us
  waiting for transfers between devices  321 us (33%)
  local copies, waits for them, and re-layouts  221 us (23%)
  blocking collectives  158 us (16%)
  matrix products  146 us (15%)
  starting transfers between devices  85.4 us (9%)
  other arithmetic  28.3 us (3%)
  between operations  14.6 us (1%)
    all_to_all x4, waiting for transfers between devices, shards(): lax.all_to_all(partial_image, 'rows', split_axis=1, concat_axis=0, tiled=...  278 us
    all_gather x4, blocking collectives, shards(): gathered_mean = lax.all_gather(current_mean, 'rows', axis=0, tiled=True)  158 us
    dot_general x4, matrix products, right_product(): jnp.einsum('rtkj,tckj->rtc', picked, shaped, precision=lax.Precision.HIGH...  85.7 us
    all_to_all x4, starting transfers between devices, shards(): lax.all_to_all(partial_image, 'rows', split_axis=1, concat_axis=0, tiled=...  84.8 us
    gather x7, local copies, waits for them, and re-layouts, right_product(): picked = tiled[:, pattern_block, :]  83.1 us
    dot_general x4, matrix products, left_product(): jnp.einsum('tkjc,tqkj->ctq', picked, shaped, precision=lax.Precision.HIGH...  59.8 us
    gather x4, local copies, waits for them, and re-layouts, left_product(): picked = tiled[pattern_block]  44.4 us
    all_gather x4, waiting for transfers between devices, shards(): lax.all_gather(gain_tiles[block_index], 'rows', axis=0, tiled=True)  41.7 us
  transfers between devices with their start and end apart: 8, of which 4 were waited for; matrix products, arithmetic and copies ran while one was open for 32% of the time, Pallas kernels for 0%

commit v1 on v0

--- a/solution.py
+++ b/solution.py
@@ -8,6 +8,30 @@
 PER_ROW = 3
 BLOCKS = 4
 TILE_ROWS = 32
+
+
+def make_pieces_all_in(message):
+    spare, z2, even = (lax.psum(1, axis_name="rows"), lax.axis_index("rows"), message.shape[0])
+    bank = tuple((ii * spare if h == 0 else ii for h, ii in enumerate(message.shape)))
+    tmp = piece_next = message
+    q_next = lax.dynamic_update_slice_in_dim(
+        jnp.zeros(bank, message.dtype), message, z2 * even, axis=0
+    )
+    for i in [*range(1, spare // 2 + 1)]:
+        tmp = lax.ppermute(
+            tmp, axis_name="rows", perm=tuple(((h, (h + 1) % spare) for h in range(spare)))
+        )
+        q_next = lax.dynamic_update_slice_in_dim(q_next, tmp, (z2 - i) % spare * even, axis=0)
+        if 2 * i < spare:
+            piece_next = lax.ppermute(
+                piece_next,
+                axis_name="rows",
+                perm=tuple(((h, (h - 1) % spare) for h in range(spare))),
+            )
+            q_next = lax.dynamic_update_slice_in_dim(
+                q_next, piece_next, (z2 + i) % spare * even, axis=0
+            )
+    return q_next
 
 
 def right_product(dense_rows, gain_values, pattern_block):
@@ -41,7 +65,7 @@
     mean_list = []
     for block_index in reversed(range(BLOCKS)):
         pattern_block = tile_pattern[block_index]
-        gain_values = lax.all_gather(gain_tiles[block_index], "rows", axis=0, tiled=True)
+        gain_values = make_pieces_all_in(gain_tiles[block_index])
         partial_image = right_product(covariance, gain_values, pattern_block)
         received = lax.all_to_all(partial_image, "rows", split_axis=1, concat_axis=0, tiled=True)
         covariance = (

time: 979 us -> 1130 us (1.15)
  the two profiles are of different devices: /device:TPU:0 before, /device:TPU:13 now
where the time goes in v1:
time: 1130 us; the launch traced here: 1120 us
  waiting for transfers between devices  414 us (37%)
  local copies, waits for them, and re-layouts  280 us (25%)
  starting transfers between devices  167 us (15%)
  matrix products  142 us (13%)
  blocking collectives  78.4 us (7%)
  other arithmetic  32.6 us (3%)
    ppermute x32, waiting for transfers between devices, make_pieces_all_in(): lax.ppermute(tmp, axis_name='rows', perm=tuple(((h, (h + 1) % spare) for...  327 us
    dot_general x4, matrix products, right_product(): jnp.einsum('rtkj,tckj->rtc', picked, shaped, precision=lax.Precision.HIGH...  82.8 us
    gather x7, local copies, waits for them, and re-layouts, right_product(): picked = tiled[:, pattern_block, :]  82.7 us
    all_gather x4, blocking collectives, shards(): gathered_mean = lax.all_gather(current_mean, 'rows', axis=0, tiled=True)  78.4 us
    all_to_all x4, waiting for transfers between devices, shards(): lax.all_to_all(partial_image, 'rows', split_axis=1, concat_axis=0, tiled=...  74.8 us
    ppermute x32, starting transfers between devices, make_pieces_all_in(): lax.ppermute(tmp, axis_name='rows', perm=tuple(((h, (h + 1) % spare) for...  73.5 us
    dot_general x4, matrix products, left_product(): jnp.einsum('tkjc,tqkj->ctq', picked, shaped, precision=lax.Precision.HIGH...  58.8 us
    ppermute x28, starting transfers between devices, make_pieces_all_in(): lax.ppermute(piece_next, axis_name='rows', perm=tuple(((h, (h - 1) % spar...  50.7 us
  transfers between devices with their start and end apart: 64, of which 31 were waited for; matrix products, arithmetic and copies ran while one was open for 13% of the time, Pallas kernels for 0%

profile of v1, /device:TPU:13, one launch (start us, length us, event | category | flops | bytes accessed | tf_op | source)
XLA Modules:
  0.0 1116.1 jit_solution(11514172593955072486)
XLA Ops:
  13.1 16.9 %all-gather = f32[16,1,256]{2,1,0:T(1,128)S(1)} all-gather(f32[1,1,256]{2,1,0:T(1,128)} %bitcast.206), channel_id=1, replica_groups=mesh['parts'=2,'rows'=16] {'rows'}, dimensions={0}, use_global_device_ids=true | all-gather | bytes 17408 | tf_op jit(solution)/shard_map/all_gather | solution.py:75
  39.2 23.8 %all-gather.1 = f32[16,1,256]{2,1,0:T(1,128)S(1)} all-gather(f32[1,1,256]{2,1,0:T(1,128)S(1)} %bitcast.199), channel_id=1, replica_groups=mesh['parts'=2,'rows'=16] {'rows'}, dimensions={0}, use_global_device_ids=true | all-gather | bytes 17408 | tf_op jit(solution)/shard_map/all_gather | solution.py:75
  71.9 18.6 %all-gather.2 = f32[16,1,256]{2,1,0:T(1,128)S(1)} all-gather(f32[1,1,256]{2,1,0:T(1,128)S(1)} %bitcast.200), channel_id=1, replica_groups=mesh['parts'=2,'rows'=16] {'rows'}, dimensions={0}, use_global_device_ids=true | all-gather | bytes 17408 | tf_op jit(solution)/shard_map/all_gather | solution.py:75
  96.9 19.0 %all-gather.3 = f32[16,1,256]{2,1,0:T(1,128)S(1)} all-gather(f32[1,1,256]{2,1,0:T(1,128)S(1)} %bitcast.201), channel_id=1, replica_groups=mesh['parts'=2,'rows'=16] {'rows'}, dimensions={0}, use_global_device_ids=true | all-gather | bytes 17408 | tf_op jit(solution)/shard_map/all_gather | solution.py:75
  118.5 5.6 copy.131
  124.1 5.6 copy.133
  129.6 11.1 gather_fusion
  160.2 11.1 collective-permute-start.58
  177.8 19.2 %fusion.6 = f32[32,128,256,1]{2,1,0,3:T(8,128)} fusion(f32[32,128,3,128]{3,1,0,2:T(8,128)S(1)} %bitcast.178, f32[32,3,256,128]{3,2,1,0:T(8,128)} %bitcast.177), kind=kOutput, calls=%fused_computation.19 | convolution fusion | flops 4831838208 | bytes 23068672 | tf_op jit(solution)/shard_map/rtkj,tckj->rtc/dot_general | solution.py:42
  197.0 5.3 copy.135
  202.4 13.0 %all-to-all-start = ((f32[256,16,256]{2,0,1:T(8,128)}), f32[256,16,256]{2,0,1:T(8,128)}, u32[]{:S(2)}, u32[]{:S(2)}) async-start(f32[256,16,256]{2,0,1:T(8,128)} %copy.135), calls=%async_computation | async-start | bytes 8388608 | tf_op jit(solution)/shard_map/all_to_all | solution.py:70
  216.9 93.4 %collective-permute-done.30 = f32[256,3,128]{2,0,1:T(8,128)S(1)} collective-permute-done((f32[256,3,128]{2,0,1:T(8,128)S(1)}, f32[256,3,128]{2,0,1:T(8,128)S(1)}, u32[]{:S(2)}, u32[]{:S(2)}) %collective-permute-start.30) | collective-permute-done | bytes 393248 | tf_op jit(solution)/shard_map/ppermute | solution.py:21
  338.3 9.8 fusion.22
  348.1 5.6 copy.137
  385.8 11.1 gather_fusion.1
  396.9 15.1 %bitcast_add_fusion = (f32[256,32,128]{0,2,1:T(8,128)}, f32[32,128,256,1]{2,1,0,3:T(8,128)}) fusion(f32[256,32,128]{0,2,1:T(8,128)} %bitcast.187, f32[32,128,3,128]{3,1,0,2:T(8,128)} %bitcast.179, f32[32,3,128,256]{3,2,1,0:T(8,128)} %bitcast.180), kind=kOutput, calls=%fused_computation.30 | convolution fusion | flops 4832886784 | bytes 31457280 | tf_op jit(solution)/shard_map/tkjc,tqkj->ctq/dot_general | solution.py:51
  411.9 11.1 gather_fusion.2
  423.0 12.7 %copy.139 = f32[32,3,256,128]{3,2,0,1:T(8,128)} copy(f32[32,3,256,128]{2,3,1,0:T(8,128)} %bitcast.174) | data formatting | bytes 25165824 | tf_op jit(solution)/shard_map/gather | solution.py:40
  435.7 21.2 %fusion.4 = f32[32,128,256,1]{2,1,0,3:T(8,128)} fusion(f32[32,128,3,128]{3,1,0,2:T(8,128)} %bitcast.5, f32[32,3,256,128]{3,2,0,1:T(8,128)} %copy.139), kind=kOutput, calls=%fused_computation.17 | convolution fusion | flops 4831838208 | bytes 23068672 | tf_op jit(solution)/shard_map/rtkj,tckj->rtc/dot_general | solution.py:42
  456.9 5.3 copy.140
  462.3 10.0 all-to-all-start.1
  473.7 93.4 %collective-permute-done.15 = f32[256,3,128]{2,0,1:T(8,128)S(1)} collective-permute-done((f32[256,3,128]{2,0,1:T(8,128)S(1)}, f32[256,3,128]{2,0,1:T(8,128)S(1)}, u32[]{:S(2)}, u32[]{:S(2)}) %collective-permute-start.15) | collective-permute-done | bytes 393248 | tf_op jit(solution)/shard_map/ppermute | solution.py:21
  595.2 5.6 copy.142
  631.9 11.1 gather_fusion.3
  643.0 15.0 %bitcast_add_fusion.1 = (f32[256,32,128]{0,2,1:T(8,128)}, f32[32,128,256,1]{2,1,0,3:T(8,128)}) fusion(f32[256,32,128]{0,2,1:T(8,128)} %bitcast.188, f32[32,128,3,128]{3,1,0,2:T(8,128)} %bitcast.5, f32[32,3,128,256]{3,2,1,0:T(8,128)} %bitcast.181), kind=kOutput, calls=%fused_computation.31 | convolution fusion | flops 4832886784 | bytes 31457280 | tf_op jit(solution)/shard_map/tkjc,tqkj->ctq/dot_general | solution.py:51
  658.0 11.1 gather_fusion.4
  669.1 12.9 %copy.144 = f32[32,3,256,128]{3,2,0,1:T(8,128)} copy(f32[32,3,256,128]{2,3,1,0:T(8,128)} %bitcast.175) | data formatting | bytes 25165824 | tf_op jit(solution)/shard_map/gather | solution.py:40
  682.0 21.2 %fusion.2 = f32[32,128,256,1]{2,1,0,3:T(8,128)} fusion(f32[32,128,3,128]{3,1,0,2:T(8,128)} %bitcast.3, f32[32,3,256,128]{3,2,0,1:T(8,128)} %copy.144), kind=kOutput, calls=%fused_computation.15 | convolution fusion | flops 4831838208 | bytes 23068672 | tf_op jit(solution)/shard_map/rtkj,tckj->rtc/dot_general | solution.py:42
  703.2 5.3 copy.145
  708.6 9.8 all-to-all-start.2
  719.9 93.4 %collective-permute-done = f32[256,3,128]{2,0,1:T(8,128)S(1)} collective-permute-done((f32[256,3,128]{2,0,1:T(8,128)S(1)}, f32[256,3,128]{2,0,1:T(8,128)S(1)}, u32[]{:S(2)}, u32[]{:S(2)}) %collective-permute-start) | collective-permute-done | bytes 393248 | tf_op jit(solution)/shard_map/ppermute | solution.py:21
  841.4 5.6 copy.147
  879.1 11.1 gather_fusion.5
  890.2 15.0 %bitcast_add_fusion.2 = (f32[256,32,128]{0,2,1:T(8,128)}, f32[32,128,256,1]{2,1,0,3:T(8,128)}) fusion(f32[256,32,128]{0,2,1:T(8,128)} %bitcast.186, f32[32,128,3,128]{3,1,0,2:T(8,128)} %bitcast.3, f32[32,3,128,256]{3,2,1,0:T(8,128)} %bitcast.182), kind=kOutput, calls=%fused_computation.32 | convolution fusion | flops 4832886784 | bytes 31457280 | tf_op jit(solution)/shard_map/tkjc,tqkj->ctq/dot_general | solution.py:51
  905.2 11.1 gather_fusion.6
  916.3 12.7 %copy.149 = f32[32,3,256,128]{3,2,0,1:T(8,128)} copy(f32[32,3,256,128]{2,3,1,0:T(8,128)} %bitcast.176) | data formatting | bytes 25165824 | tf_op jit(solution)/shard_map/gather | solution.py:40
  929.1 21.2 %fusion = f32[32,128,256,1]{2,1,0,3:T(8,128)} fusion(f32[32,128,3,128]{3,1,0,2:T(8,128)} %bitcast.1, f32[32,3,256,128]{3,2,0,1:T(8,128)} %copy.149), kind=kOutput, calls=%fused_computation.13 | convolution fusion | flops 4831838208 | bytes 23068672 | tf_op jit(solution)/shard_map/rtkj,tckj->rtc/dot_general | solution.py:42
  950.3 5.3 copy.150
  955.6 10.3 all-to-all-start.3
  966.6 5.6 copy.155
  972.2 5.6 copy.154
  977.9 5.6 copy.153
  983.4 74.8 %all-to-all-done.3 = f32[256,16,256]{2,0,1:T(8,128)} async-done(((f32[256,16,256]{2,0,1:T(8,128)}), f32[256,16,256]{2,0,1:T(8,128)}, u32[]{:S(2)}, u32[]{:S(2)}) %all-to-all-start.3) | async-done | bytes 4194336 | tf_op jit(solution)/shard_map/all_to_all | solution.py:70
  1058.2 11.1 gather_fusion.7
  1069.3 13.8 %fusion.8 = f32[32,128,256,1]{2,1,0,3:T(8,128)} fusion(f32[32,128,3,128]{3,1,0,2:T(8,128)} %bitcast.1, f32[32,3,128,256]{3,2,1,0:T(8,128)} %bitcast.183), kind=kOutput, calls=%fused_computation.21 | convolution fusion | flops 4831838208 | bytes 23068672 | tf_op jit(solution)/shard_map/tkjc,tqkj->ctq/dot_general | solution.py:51
  1083.1 5.6 copy.152
  1088.7 16.3 %slice_add_fusion = (f32[1,256,4096]{2,1,0:T(8,128)S(1)}, f32[1,256,4096]{2,1,0:T(8,128)}, f32[1,256,4096]{2,1,0:T(8,128)}, f32[1,256,4096]{2,1,0:T(8,128)}) fusion(f32[1,256,4096]{2,1,0:T(8,128)} %copy.152, f32[4,256,4096]{2,1,0:T(8,128)} %param.11, f32[1,256,4096]{2,1,0:T(8,128)} %copy.155, f32[1,256,4096]{2,1,0:T(8,128)} %copy.154, f32[1,256,4096]{2,1,0:T(8,128)} %copy.153), kind=kLoop, calls=%fused_computation.33 | loop fusion | flops 4194304 | bytes 50331648 | tf_op jit(solution)/shard_map/add | solution.py:72
  1105.0 10.7 pad_maximum_fusion
  (277 shorter events, 249.3 us)
Async XLA Ops:
  4.8 31.3 %collective-permute-start.46 = (f32[256,3,128]{2,0,1:T(8,128)S(1)}, f32[256,3,128]{2,0,1:T(8,128)}, u32[]{:S(2)}, u32[]{:S(2)}) collective-permute-start(f32[256,3,128]{2,0,1:T(8,128)S(1)} %get-tuple-element.23), channel_id=1, source_target_pairs={{0,15},{1,0},{2,1},{3,2},{4,3},{5,4},{6,5},{7,6},{8,7},{9,8},{10,9... | collective-permute-start | bytes 1179656 | tf_op jit(solution)/shard_map/ppermute | solution.py:26
  9.6 27.1 %collective-permute-start.47 = (f32[256,3,128]{2,0,1:T(8,128)}, f32[256,3,128]{2,0,1:T(8,128)}, u32[]{:S(2)}, u32[]{:S(2)}) collective-permute-start(f32[256,3,128]{2,0,1:T(8,128)} %collective-permute-done.45), channel_id=1, source_target_pairs={{0,1},{1,2},{2,3},{3,4},{4,5},{5,6},{6,7},{7,8},{8,9},{9,10},{10,1... | collective-permute-start | bytes 1179656 | tf_op jit(solution)/shard_map/ppermute | solution.py:21
  36.1 33.0 %collective-permute-start.48 = (f32[256,3,128]{2,0,1:T(8,128)}, f32[256,3,128]{2,0,1:T(8,128)S(1)}, u32[]{:S(2)}, u32[]{:S(2)}) collective-permute-start(f32[256,3,128]{2,0,1:T(8,128)} %collective-permute-done.46), channel_id=1, source_target_pairs={{0,15},{1,0},{2,1},{3,2},{4,3},{5,4},{6,5},{7,6},{8,7},{9,8},{10,9... | collective-permute-start | bytes 1179656 | tf_op jit(solution)/shard_map/ppermute | solution.py:26
  36.7 32.7 %collective-permute-start.49 = (f32[256,3,128]{2,0,1:T(8,128)}, f32[256,3,128]{2,0,1:T(8,128)}, u32[]{:S(2)}, u32[]{:S(2)}) collective-permute-start(f32[256,3,128]{2,0,1:T(8,128)} %collective-permute-done.47), channel_id=1, source_target_pairs={{0,1},{1,2},{2,3},{3,4},{4,5},{5,6},{6,7},{7,8},{8,9},{9,10},{10,1... | collective-permute-start | bytes 1179656 | tf_op jit(solution)/shard_map/ppermute | solution.py:21
  69.1 27.2 %collective-permute-start.50 = (f32[256,3,128]{2,0,1:T(8,128)S(1)}, f32[256,3,128]{2,0,1:T(8,128)}, u32[]{:S(2)}, u32[]{:S(2)}) collective-permute-start(f32[256,3,128]{2,0,1:T(8,128)S(1)} %collective-permute-done.48), channel_id=1, source_target_pairs={{0,15},{1,0},{2,1},{3,2},{4,3},{5,4},{6,5},{7,6},{8,7},{9,8},{10,9... | collective-permute-start | bytes 1179656 | tf_op jit(solution)/shard_map/ppermute | solution.py:26
  69.4 71.4 %collective-permute-start.51 = (f32[256,3,128]{2,0,1:T(8,128)}, f32[256,3,128]{2,0,1:T(8,128)}, u32[]{:S(2)}, u32[]{:S(2)}) collective-permute-start(f32[256,3,128]{2,0,1:T(8,128)} %collective-permute-done.49), channel_id=1, source_target_pairs={{0,1},{1,2},{2,3},{3,4},{4,5},{5,6},{6,7},{7,8},{8,9},{9,10},{10,1... | collective-permute-start | bytes 1179656 | tf_op jit(solution)/shard_map/ppermute | solution.py:21
  96.4 47.1 %collective-permute-start.52 = (f32[256,3,128]{2,0,1:T(8,128)}, f32[256,3,128]{2,0,1:T(8,128)}, u32[]{:S(2)}, u32[]{:S(2)}) collective-permute-start(f32[256,3,128]{2,0,1:T(8,128)} %collective-permute-done.50), channel_id=1, source_target_pairs={{0,15},{1,0},{2,1},{3,2},{4,3},{5,4},{6,5},{7,6},{8,7},{9,8},{10,9... | collective-permute-start | bytes 1179656 | tf_op jit(solution)/shard_map/ppermute | solution.py:26
  143.5 8.5 collective-permute-start.54
  146.3 10.4 collective-permute-start.55
  156.8 14.6 %collective-permute-start.57 = (f32[256,3,128]{2,0,1:T(8,128)S(1)}, f32[256,3,128]{2,0,1:T(8,128)S(1)}, u32[]{:S(2)}, u32[]{:S(2)}) collective-permute-start(f32[256,3,128]{2,0,1:T(8,128)S(1)} %collective-permute-done.55), channel_id=1, source_target_pairs={{0,1},{1,2},{2,3},{3,4},{4,5},{5,6},{6,7},{7,8},{8,9},{9,10},{10,1... | collective-permute-start | bytes 1179656 | tf_op jit(solution)/shard_map/ppermute | solution.py:21
  160.2 12.5 %collective-permute-start.58 = (f32[256,3,128]{2,0,1:T(8,128)S(1)}, f32[256,3,128]{2,0,1:T(8,128)S(1)}, u32[]{:S(2)}, u32[]{:S(2)}) collective-permute-start(f32[256,3,128]{2,0,1:T(8,128)S(1)} %collective-permute-done.56), channel_id=1, source_target_pairs={{0,15},{1,0},{2,1},{3,2},{4,3},{5,4},{6,5},{7,6},{8,7},{9,8},{10,9... | collective-permute-start | bytes 1179656 | tf_op jit(solution)/shard_map/ppermute | solution.py:26
  202.4 183.4 %all-to-all-start = ((f32[256,16,256]{2,0,1:T(8,128)}), f32[256,16,256]{2,0,1:T(8,128)}, u32[]{:S(2)}, u32[]{:S(2)}) async-start(f32[256,16,256]{2,0,1:T(8,128)} %copy.135), calls=%async_computation | async-start | bytes 8388608 | tf_op jit(solution)/shard_map/all_to_all | solution.py:70
  215.4 94.9 %collective-permute-start.30 = (f32[256,3,128]{2,0,1:T(8,128)S(1)}, f32[256,3,128]{2,0,1:T(8,128)S(1)}, u32[]{:S(2)}, u32[]{:S(2)}) collective-permute-start(f32[256,3,128]{2,0,1:T(8,128)S(1)} %copy-done.4), channel_id=1, source_target_pairs={{0,1},{1,2},{2,3},{3,4},{4,5},{5,6},{6,7},{7,8},{8,9},{9,10},{10,1... | collective-permute-start | bytes 1179656 | tf_op jit(solution)/shard_map/ppermute | solution.py:21
  216.9 96.8 %collective-permute-start.31 = (f32[256,3,128]{2,0,1:T(8,128)S(1)}, f32[256,3,128]{2,0,1:T(8,128)S(1)}, u32[]{:S(2)}, u32[]{:S(2)}) collective-permute-start(f32[256,3,128]{2,0,1:T(8,128)S(1)} %copy-done.4), channel_id=1, source_target_pairs={{0,15},{1,0},{2,1},{3,2},{4,3},{5,4},{6,5},{7,6},{8,7},{9,8},{10,9... | collective-permute-start | bytes 1179656 | tf_op jit(solution)/shard_map/ppermute | solution.py:26
  313.7 8.2 collective-permute-start.33
  318.5 8.2 collective-permute-start.34
  321.9 8.2 collective-permute-start.35
  326.7 8.2 collective-permute-start.36
  330.1 24.6 %collective-permute-start.37 = (f32[256,3,128]{2,0,1:T(8,128)S(1)}, f32[256,3,128]{2,0,1:T(8,128)S(1)}, u32[]{:S(2)}, u32[]{:S(2)}) collective-permute-start(f32[256,3,128]{2,0,1:T(8,128)S(1)} %collective-permute-done.35), channel_id=1, source_target_pairs={{0,15},{1,0},{2,1},{3,2},{4,3},{5,4},{6,5},{7,6},{8,7},{9,8},{10,9... | collective-permute-start | bytes 1179656 | tf_op jit(solution)/shard_map/ppermute | solution.py:26
  334.9 21.4 %collective-permute-start.38 = (f32[256,3,128]{2,0,1:T(8,128)S(1)}, f32[256,3,128]{2,0,1:T(8,128)}, u32[]{:S(2)}, u32[]{:S(2)}) collective-permute-start(f32[256,3,128]{2,0,1:T(8,128)S(1)} %collective-permute-done.36), channel_id=1, source_target_pairs={{0,1},{1,2},{2,3},{3,4},{4,5},{5,6},{6,7},{7,8},{8,9},{9,10},{10,1... | collective-permute-start | bytes 1179656 | tf_op jit(solution)/shard_map/ppermute | solution.py:21
  356.3 8.4 collective-permute-start.40
  363.0 8.2 collective-permute-start.41
  364.7 11.5 %collective-permute-start.42 = (f32[256,3,128]{2,0,1:T(8,128)S(1)}, f32[256,3,128]{2,0,1:T(8,128)S(1)}, u32[]{:S(2)}, u32[]{:S(2)}) collective-permute-start(f32[256,3,128]{2,0,1:T(8,128)S(1)} %collective-permute-done.40), channel_id=1, source_target_pairs={{0,1},{1,2},{2,3},{3,4},{4,5},{5,6},{6,7},{7,8},{8,9},{9,10},{10,1... | collective-permute-start | bytes 1179656 | tf_op jit(solution)/shard_map/ppermute | solution.py:21
  376.1 8.9 collective-permute-start.44
  462.3 169.6 %all-to-all-start.1 = ((f32[256,16,256]{2,0,1:T(8,128)}), f32[256,16,256]{2,0,1:T(8,128)}, u32[]{:S(2)}, u32[]{:S(2)}) async-start(f32[256,16,256]{2,0,1:T(8,128)} %copy.140), calls=%async_computation.1 | async-start | bytes 8388608 | tf_op jit(solution)/shard_map/all_to_all | solution.py:70
  472.2 94.9 %collective-permute-start.15 = (f32[256,3,128]{2,0,1:T(8,128)S(1)}, f32[256,3,128]{2,0,1:T(8,128)S(1)}, u32[]{:S(2)}, u32[]{:S(2)}) collective-permute-start(f32[256,3,128]{2,0,1:T(8,128)S(1)} %copy-done.3), channel_id=1, source_target_pairs={{0,1},{1,2},{2,3},{3,4},{4,5},{5,6},{6,7},{7,8},{8,9},{9,10},{10,1... | collective-permute-start | bytes 1179656 | tf_op jit(solution)/shard_map/ppermute | solution.py:21
  473.7 96.8 %collective-permute-start.16 = (f32[256,3,128]{2,0,1:T(8,128)S(1)}, f32[256,3,128]{2,0,1:T(8,128)S(1)}, u32[]{:S(2)}, u32[]{:S(2)}) collective-permute-start(f32[256,3,128]{2,0,1:T(8,128)S(1)} %copy-done.3), channel_id=1, source_target_pairs={{0,15},{1,0},{2,1},{3,2},{4,3},{5,4},{6,5},{7,6},{8,7},{9,8},{10,9... | collective-permute-start | bytes 1179656 | tf_op jit(solution)/shard_map/ppermute | solution.py:26
  570.6 8.2 collective-permute-start.18
  575.3 8.2 collective-permute-start.19
  578.8 8.2 collective-permute-start.20
  587.0 14.8 %collective-permute-start.22 = (f32[256,3,128]{2,0,1:T(8,128)S(1)}, f32[256,3,128]{2,0,1:T(8,128)S(1)}, u32[]{:S(2)}, u32[]{:S(2)}) collective-permute-start(f32[256,3,128]{2,0,1:T(8,128)S(1)} %collective-permute-done.20), channel_id=1, source_target_pairs={{0,15},{1,0},{2,1},{3,2},{4,3},{5,4},{6,5},{7,6},{8,7},{9,8},{10,9... | collective-permute-start | bytes 1179656 | tf_op jit(solution)/shard_map/ppermute | solution.py:26
  591.7 10.8 collective-permute-start.23
  601.8 8.2 collective-permute-start.24
  602.6 9.7 collective-permute-start.25
  612.2 11.5 %collective-permute-start.27 = (f32[256,3,128]{2,0,1:T(8,128)S(1)}, f32[256,3,128]{2,0,1:T(8,128)S(1)}, u32[]{:S(2)}, u32[]{:S(2)}) collective-permute-start(f32[256,3,128]{2,0,1:T(8,128)S(1)} %collective-permute-done.25), channel_id=1, source_target_pairs={{0,1},{1,2},{2,3},{3,4},{4,5},{5,6},{6,7},{7,8},{8,9},{9,10},{10,1... | collective-permute-start | bytes 1179656 | tf_op jit(solution)/shard_map/ppermute | solution.py:21
  618.1 8.2 collective-permute-start.28
  708.6 170.5 %all-to-all-start.2 = ((f32[256,16,256]{2,0,1:T(8,128)}), f32[256,16,256]{2,0,1:T(8,128)}, u32[]{:S(2)}, u32[]{:S(2)}) async-start(f32[256,16,256]{2,0,1:T(8,128)} %copy.145), calls=%async_computation.2 | async-start | bytes 8388608 | tf_op jit(solution)/shard_map/all_to_all | solution.py:70
  718.4 94.9 %collective-permute-start = (f32[256,3,128]{2,0,1:T(8,128)S(1)}, f32[256,3,128]{2,0,1:T(8,128)S(1)}, u32[]{:S(2)}, u32[]{:S(2)}) collective-permute-start(f32[256,3,128]{2,0,1:T(8,128)S(1)} %get-tuple-element.21), channel_id=1, source_target_pairs={{0,1},{1,2},{2,3},{3,4},{4,5},{5,6},{6,7},{7,8},{8,9},{9,10},{10,1... | collective-permute-start | bytes 1179656 | tf_op jit(solution)/shard_map/ppermute | solution.py:21
  719.9 96.8 %collective-permute-start.1 = (f32[256,3,128]{2,0,1:T(8,128)S(1)}, f32[256,3,128]{2,0,1:T(8,128)S(1)}, u32[]{:S(2)}, u32[]{:S(2)}) collective-permute-start(f32[256,3,128]{2,0,1:T(8,128)S(1)} %get-tuple-element.21), channel_id=1, source_target_pairs={{0,15},{1,0},{2,1},{3,2},{4,3},{5,4},{6,5},{7,6},{8,7},{9,8},{10,9... | collective-permute-start | bytes 1179656 | tf_op jit(solution)/shard_map/ppermute | solution.py:26
  821.5 8.2 collective-permute-start.4
  829.7 8.2 collective-permute-start.6
  833.2 16.1 %collective-permute-start.7 = (f32[256,3,128]{2,0,1:T(8,128)S(1)}, f32[256,3,128]{2,0,1:T(8,128)S(1)}, u32[]{:S(2)}, u32[]{:S(2)}) collective-permute-start(f32[256,3,128]{2,0,1:T(8,128)S(1)} %collective-permute-done.5), channel_id=1, source_target_pairs={{0,15},{1,0},{2,1},{3,2},{4,3},{5,4},{6,5},{7,6},{8,7},{9,8},{10,9... | collective-permute-start | bytes 1179656 | tf_op jit(solution)/shard_map/ppermute | solution.py:26
  837.9 12.1 %collective-permute-start.8 = (f32[256,3,128]{2,0,1:T(8,128)S(1)}, f32[256,3,128]{2,0,1:T(8,128)S(1)}, u32[]{:S(2)}, u32[]{:S(2)}) collective-permute-start(f32[256,3,128]{2,0,1:T(8,128)S(1)} %collective-permute-done.6), channel_id=1, source_target_pairs={{0,1},{1,2},{2,3},{3,4},{4,5},{5,6},{6,7},{7,8},{8,9},{9,10},{10,1... | collective-permute-start | bytes 1179656 | tf_op jit(solution)/shard_map/ppermute | solution.py:21
  849.3 8.2 collective-permute-start.9
  850.1 9.4 collective-permute-start.10
  859.5 11.5 %collective-permute-start.12 = (f32[256,3,128]{2,0,1:T(8,128)S(1)}, f32[256,3,128]{2,0,1:T(8,128)S(1)}, u32[]{:S(2)}, u32[]{:S(2)}) collective-permute-start(f32[256,3,128]{2,0,1:T(8,128)S(1)} %collective-permute-done.10), channel_id=1, source_target_pairs={{0,1},{1,2},{2,3},{3,4},{4,5},{5,6},{6,7},{7,8},{8,9},{9,10},{10,1... | collective-permute-start | bytes 1179656 | tf_op jit(solution)/shard_map/ppermute | solution.py:21
  865.6 8.2 collective-permute-start.13
  955.6 102.6 %all-to-all-start.3 = ((f32[256,16,256]{2,0,1:T(8,128)}), f32[256,16,256]{2,0,1:T(8,128)}, u32[]{:S(2)}, u32[]{:S(2)}) async-start(f32[256,16,256]{2,0,1:T(8,128)} %copy.150), calls=%async_computation.3 | async-start | bytes 8388608 | tf_op jit(solution)/shard_map/all_to_all | solution.py:70
  (36 other events, 468.6 us)
